TPU v7x, 32 devices: a whole 2x2x4 slice. The times are simulated.
32 devices in a mesh: chan: 8 (over y, x, core), tile: 4 (over z).
Axes of the slice: x: 2, y: 2, z: 4, core: 2. Of those that a mesh axis runs over, the one named last changes fastest.
Arguments:
- voltages: bfloat16 [4, 16, 555008], P('tile', 'chan'), may hold values from -6 to 6
- fir_taps: float32 [16, 2048], replicated, may hold values from -4 to 4
- channels: int32 [8], replicated, may hold values from 0 to 2047
- input_good_mask: int32 [4, 16], P('tile', 'chan'), may hold values 0 or 1
- tile_map: int32 [8, 4], replicated, may hold values from 0 to 3, each once within a row
Outputs:
- visibilities: bfloat16 [8, 4, 2, 32, 32], P('chan', 'tile')
Inputs may be any that keep to these rules, and one draw needn't show every extreme that they name: `tile_map`: for every channel, every tile of the 2 x 2 grid, numbered row by row, stands in exactly one slot.
All inputs are finite; a program needn't handle non-finite values. No bound on the sum of `input_good_mask` on one device may be relied on, other than what follows from the above.
Results may differ from a plain program's by a relative error of at most 0.0077.
Values may be sent and summed in bfloat16 or wider, within the bound.
No kernel may reach another device: no remote copies, remote signals or barrier semaphores. Data moves between devices by JAX's collectives and lax.ppermute only.
A program may use at most 64 MiB of HBM per device.

v0:
```python
import functools
import math

import jax
import jax.numpy as jnp
from jax import lax
from jax.experimental import pallas as pl
from jax.experimental.pallas import tpu as pltpu
from jax.sharding import PartitionSpec as P

TRANSFORM_LENGTH = 2048
FILTER_TAPS = 16
SPECTRA_SUMMED = 256
FRAMES = SPECTRA_SUMMED + FILTER_TAPS - 1
ROWS = 272
LANES = 128
BLOCKS = TRANSFORM_LENGTH // LANES
DIRECT = 10
HALVES = SPECTRA_SUMMED // LANES
OCTANT = TRANSFORM_LENGTH // 8


def cos_sin(phase):
    turns = (phase + OCTANT) >> (OCTANT.bit_length())
    angle = (phase - (turns << OCTANT.bit_length())).astype(jnp.float32) * (2.0 * math.pi / TRANSFORM_LENGTH)
    square = angle * angle
    cosine, sine = jnp.zeros_like(angle), jnp.zeros_like(angle)
    for power in range(10, -1, -2):
        sign = -1.0 if power % 4 else 1.0
        cosine = cosine * square + sign / math.factorial(power)
        sine = sine * square + sign / math.factorial(power + 1)
    sine = sine * angle
    odd = (turns & 1) == 1
    first, second = jnp.where(odd, sine, cosine), jnp.where(odd, cosine, sine)
    first = jnp.where(((turns + 1) & 2) == 2, -first, first)
    second = jnp.where((turns & 2) == 2, -second, second)
    return first, second


def parity(place):
    return (place ^ (place >> 1) ^ (place >> 2)) & 1


def dft_blocks(chans, channels_ref):
    lane = lax.broadcasted_iota(jnp.int32, (chans, LANES), 1)
    place = lax.broadcasted_iota(jnp.int32, (chans, chans), 0)
    source = lax.broadcasted_iota(jnp.int32, (chans, chans), 1)
    turned = jnp.where(source == ((place + chans - 2) & (chans - 1)), channels_ref[...], 0)
    channel = jnp.sum(turned.astype(jnp.float32), axis=1, keepdims=True).astype(jnp.int32)
    channel = jnp.broadcast_to(channel, (chans, LANES))

    def unit(phase):
        return cos_sin(phase & (TRANSFORM_LENGTH - 1))

    factor = 1.0 / math.sqrt(TRANSFORM_LENGTH)
    cos0, sin0 = unit(channel * lane)
    blocks = [(cos0 * factor, sin0 * factor)]
    for bit in range(BLOCKS.bit_length() - 1):
        cos1, sin1 = unit(channel * (LANES << bit))
        blocks += [(c * cos1 - s * sin1, s * cos1 + c * sin1) for c, s in blocks]
    return [jnp.concatenate([cosine, -sine], axis=0) for cosine, sine in blocks]


def build_table(chans, blocks, taps_ref, table_ref):
    for nb, dft in enumerate(blocks):
        columns = slice(nb * LANES, (nb + 1) * LANES)
        for tap in range(FILTER_TAPS):
            table_ref[tap * 2 * chans : (tap + 1) * 2 * chans, columns] = (
                dft * taps_ref[tap : tap + 1, columns]
            ).astype(jnp.bfloat16)


def front_kernel(
    own, chans, copies, channels_hbm, mask_hbm, taps_hbm, x_hbm, out_ref,
    channels_ref, mask_ref, taps_ref, x_ref, rest_ref, sorted_ref, table_ref, fold_ref, block_ref,
    sems, small_sems,
):
    small = [
        pltpu.make_async_copy(source, target, small_sems.at[place])
        for place, (source, target) in enumerate(
            ((taps_hbm, taps_ref), (channels_hbm, channels_ref), (mask_hbm, mask_ref))
        )
    ]
    transfers = [
        pltpu.make_async_copy(x_hbm.at[:, nb], x_ref.at[nb, pl.ds(0, FRAMES)], sems.at[nb])
        for nb in range(DIRECT)
    ]
    halves = ((0, ROWS // 2), (ROWS // 2, FRAMES))
    rest = [
        pltpu.make_async_copy(
            x_hbm.at[pl.ds(start, stop - start), pl.ds(DIRECT, BLOCKS - DIRECT)],
            rest_ref.at[pl.ds(start, stop - start)],
            sems.at[DIRECT + part],
        )
        for part, (start, stop) in enumerate(halves)
    ]
    for transfer in small:
        transfer.start()
    for place, transfer in enumerate(rest + transfers):
        transfer.start(priority=place % 2)
    small[1].wait()
    blocks = dft_blocks(chans, channels_ref)
    small[0].wait()
    small[2].wait()
    build_table(chans, blocks, taps_ref, table_ref)
    for part, transfer in enumerate(rest):
        transfer.wait()
        frames = pl.ds(part * (ROWS // 2), ROWS // 2)
        lines = pl.ds(part * (ROWS // 2) * own, ROWS // 2 * own)
        for place in range(BLOCKS - DIRECT):
            sorted_ref[place, lines, :] = rest_ref[frames, place].reshape(ROWS // 2 * own, LANES)
    rows_ref = x_ref.reshape(DIRECT, ROWS * own, LANES)
    for transfer in transfers:
        transfer.wait()
    product = lax.dot_general(
        jnp.concatenate(
            [rows_ref[nb] for nb in range(DIRECT)]
            + [sorted_ref[place] for place in range(BLOCKS - DIRECT)],
            axis=1,
        ),
        table_ref[...],
        (((1,), (1,)), ((), ())),
        preferred_element_type=jnp.float32,
    )
    kinds = 2 * chans
    together = LANES // kinds
    kept = -(-(SPECTRA_SUMMED + together - 1) // 8) * 8
    folded = product[: kept * own, :LANES]
    for group in range(1, FILTER_TAPS // together):
        start = group * together * own
        folded = folded + product[
            start : start + kept * own, group * LANES : (group + 1) * LANES
        ]
    fold_ref[: kept * own, :] = folded
    for i in range(own):
        turned = fold_ref[pl.ds(i, fold_ref.shape[0] // own, stride=own), :].T
        spectra = turned[:kinds, :SPECTRA_SUMMED]
        for tap in range(1, together):
            shifted = pltpu.roll(
                turned[tap * kinds : (tap + 1) * kinds, :], turned.shape[1] - tap, axis=1
            )
            spectra = spectra + shifted[:, :SPECTRA_SUMMED]
        spectra = spectra * mask_ref[0, i].astype(jnp.float32)
        for half in range(HALVES):
            for q in range(2):
                block_ref[pl.ds((i * HALVES + half) * 2 + q, chans, stride=4 * own), :] = spectra[
                    q * chans : (q + 1) * chans, half * LANES : (half + 1) * LANES
                ]
    block = block_ref[...].astype(jnp.bfloat16)
    for copy in range(copies):
        out_ref[copy] = block


def back_kernel(
    own, grid_side, tile_map_ref, mine_ref, other_ref, out_ref, wide_ref, signal_ref
):
    slot = lax.broadcasted_iota(jnp.int32, tile_map_ref.shape, 0)
    owner = lax.broadcasted_iota(jnp.int32, tile_map_ref.shape, 1)
    wanted = (slot == lax.axis_index("tile")) & (owner == lax.axis_index("chan"))
    tile = jnp.sum(jnp.where(wanted, tile_map_ref[...].astype(jnp.float32), 0.0)).astype(jnp.int32)
    sources = mine_ref.shape[0]
    inputs = sources * 2 * own
    side = inputs // grid_side
    lines = mine_ref.shape[1] // 2
    pitch = lines + 1
    chan = lax.axis_index("chan")
    core_here = chan & 1
    place_here = lax.axis_index("tile") * (lax.axis_size("chan") // 2) + (chan >> 1)
    group_here = core_here ^ parity(place_here)

    def my_channel(blocks_ref, block):
        both = blocks_ref[block].astype(jnp.float32)
        return jnp.where(core_here == 0, both[:lines], both[lines:])

    for block in range(sources):
        place = (block - 1) % sources
        first_is_mine = group_here == parity(place)
        mine, other = my_channel(mine_ref, block), my_channel(other_ref, block)
        target = pl.ds(place * pitch, lines)
        wide_ref[0, target, :] = jnp.where(first_is_mine, mine, other)
        wide_ref[1, target, :] = jnp.where(first_is_mine, other, mine)
    for core in range(2):
        for i in range(own):
            for half in range(HALVES):
                for q in range(2):
                    line = (i * HALVES + half) * 2 + q
                    target = pl.ds(core * own + i, sources, stride=2 * own)
                    signal_ref[q * HALVES + half, target, :] = wide_ref[
                        core, pl.ds(line, sources, stride=pitch), :
                    ]
    bits = grid_side.bit_length() - 1
    row_start = pl.multiple_of((tile >> bits) * side, side)
    col_start = pl.multiple_of((tile & (grid_side - 1)) * side, side)

    def inputs_from(start):
        planes = [signal_ref[plane, pl.ds(start, side), :] for plane in range(2 * HALVES)]
        return jnp.concatenate(planes, axis=1).astype(jnp.bfloat16)

    rows, cols = inputs_from(row_start), inputs_from(col_start)
    turned = jnp.concatenate([-rows[:, SPECTRA_SUMMED:], rows[:, :SPECTRA_SUMMED]], axis=1)
    product = lax.dot_general(
        jnp.concatenate([rows, turned], axis=0), cols, (((1,), (1,)), ((), ())),
        preferred_element_type=jnp.float32,
    )
    visible = (product * (1.0 / SPECTRA_SUMMED)).astype(jnp.bfloat16)
    for part in range(2):
        out_ref[0, 0, part] = visible[part * side : (part + 1) * side]


def on_device(voltages, fir_taps, channels, input_good_mask, tile_map):
    own = voltages.shape[1]
    chans = channels.shape[0]
    n_chan = lax.axis_size("chan")
    n_tile = lax.axis_size("tile")
    assert chans == n_chan and 2 * chans <= LANES and n_chan & (n_chan - 1) == 0
    chips = n_chan // 2
    order = [n_tile * chips - 1] + list(range(n_tile * chips - 1))
    groups = [[2 * place + (parity(place) ^ group) for place in order] for group in range(2)]
    x = voltages.reshape(own, FRAMES, BLOCKS, LANES).transpose(1, 2, 0, 3)
    operands = (channels.reshape(1, chans), input_good_mask, fir_taps, x)
    hbm = pl.BlockSpec(memory_space=pltpu.HBM)
    vmem = pl.BlockSpec(memory_space=pltpu.VMEM)
    per_block = 2 * HALVES * own
    kinds = 2 * chans
    folded_rows = SPECTRA_SUMMED + (LANES if kinds < LANES else 0)
    spectra = pl.pallas_call(
        functools.partial(front_kernel, own, chans, n_tile),
        out_shape=pltpu.VMEM((n_tile, chans * per_block, LANES), jnp.bfloat16),
        in_specs=[hbm, hbm, hbm, hbm],
        out_specs=vmem,
        scratch_shapes=[
            pltpu.VMEM((1, chans), jnp.int32),
            pltpu.SMEM(input_good_mask.shape, jnp.int32),
            pltpu.VMEM(fir_taps.shape, jnp.float32),
            pltpu.VMEM((DIRECT, ROWS, own, LANES), jnp.bfloat16),
            pltpu.VMEM((ROWS, BLOCKS - DIRECT, own, LANES), jnp.bfloat16),
            pltpu.VMEM((BLOCKS - DIRECT, ROWS * own, LANES), jnp.bfloat16),
            pltpu.VMEM((FILTER_TAPS * kinds, TRANSFORM_LENGTH), jnp.bfloat16),
            pltpu.VMEM((own * folded_rows, LANES), jnp.float32),
            pltpu.VMEM((chans * per_block, LANES), jnp.float32),
            pltpu.SemaphoreType.DMA((DIRECT + 2,)),
            pltpu.SemaphoreType.DMA((3,)),
        ],
        compiler_params=pltpu.CompilerParams(vmem_limit_bytes=32 << 20),
        name="front",
    )(*(pltpu.with_memory_space_constraint(v, pltpu.HBM) for v in operands))
    spectra = spectra.reshape(n_tile * chips, 2 * per_block, LANES)
    mine = lax.all_to_all(
        spectra, ("tile", "chan"), split_axis=0, concat_axis=0, axis_index_groups=groups, tiled=True
    )
    other = lax.ppermute(mine, "chan", [(c, c ^ 1) for c in range(n_chan)])
    grid_side = n_tile // 8 + 2
    inputs = n_tile * n_chan * own
    side = inputs // grid_side
    return pl.pallas_call(
        functools.partial(back_kernel, own, grid_side),
        out_shape=jax.ShapeDtypeStruct((1, 1, 2, side, side), jnp.bfloat16),
        in_specs=[vmem, vmem, vmem],
        out_specs=vmem,
        scratch_shapes=[
            pltpu.VMEM((2, n_tile * chips * (per_block + 1), LANES), jnp.float32),
            pltpu.VMEM((2 * HALVES, inputs, LANES), jnp.float32),
        ],
        compiler_params=pltpu.CompilerParams(vmem_limit_bytes=(4 << 20) + 60 * inputs * LANES * own),
        name="back",
    )(tile_map.T, mine, other)


def solution(mesh):
    in_specs = (P("tile", "chan", None), P(), P(), P("tile", "chan"), P())
    out_specs = P("chan", "tile", None, None, None)
    return jax.shard_map(
        on_device, mesh=mesh, in_specs=in_specs, out_specs=out_specs, check_vma=False
    )
```

profile of v0, /device:TPU:0, one launch (start us, length us, event | category | flops | bytes accessed | tf_op | source)
XLA Modules:
  0.0 17.7 jit_solution(17646861707192205522)
XLA Ops:
  0.0 0.0 copy-start
  0.0 3.3 %front.1 = bf16[4,64,128]{2,1,0:T(8,128)(2,1)S(1)} custom-call(s32[1,8]{1,0:T(1,128)} %bitcast.9, s32[1,2]{1,0:T(1,128)} %mask_hbm.1, f32[16,2048]{1,0:T(8,128)} %taps_hbm.1, bf16[271,16,2,128]{3,2,1,0:T(2,128)(2,1)} %bitcast.8), custom_call_target="tpu_custom_call" | custom-call | tf_op jit(solution)/shard_map/front/pallas_call | solution.py:226
  3.4 12.2 %all_to_all.5.mine_ref = bf16[16,16,128]{2,1,0:T(8,128)(2,1)S(1)} all-to-all(bf16[16,16,128]{2,1,0:T(8,128)(2,1)S(1)} %bitcast.6), channel_id=1, replica_groups={{31,0,12,20,24,5,9,17,29,2,14,22,26,7,11,19},{27,4,8,16,28,1,13,21,25,6..., dimensions={0} | all-to-all | bytes 131072 | tf_op jit(solution)/shard_map/all_to_all | solution.py:248
  15.6 0.1 collective-permute-start
  15.7 1.1 %collective-permute-done.other_ref = bf16[16,16,128]{2,1,0:T(8,128)(2,1)S(1)} collective-permute-done((bf16[16,16,128]{2,1,0:T(8,128)(2,1)S(1)}, bf16[16,16,128]{2,1,0:T(8,128)(2,1)S(1)}, u32[]{:S(2)}, u32[]{:S(2)}) %collective-permute-start) | collective-permute-done | bytes 65568 | tf_op jit(solution)/shard_map/ppermute | solution.py:251
  16.8 0.0 copy-done
  16.8 0.9 %back.1 = bf16[1,1,2,32,32]{4,3,2,1,0:T(8,128)(2,1)} custom-call(s32[4,8]{1,0:T(4,128)S(1)} %bitcast.7, bf16[16,16,128]{2,1,0:T(8,128)(2,1)S(1)} %all_to_all.5.mine_ref, bf16[16,16,128]{2,1,0:T(8,128)(2,1)S(1)} %collective-permute-done.other_ref), custom_call_target="tpu_custom_call" | custom-call | tf_op jit(solution)/shard_map/back/pallas_call | solution.py:255
Async XLA Ops:
  0.0 16.8 %copy-start = (s32[8,4]{0,1:T(4,128)S(1)}, s32[8,4]{0,1:T(4,128)}, u32[]{:S(2)}) copy-start(s32[8,4]{0,1:T(4,128)} %param.9) | copy-start | bytes 388
  15.6 1.3 %collective-permute-start = (bf16[16,16,128]{2,1,0:T(8,128)(2,1)S(1)}, bf16[16,16,128]{2,1,0:T(8,128)(2,1)S(1)}, u32[]{:S(2)}, u32[]{:S(2)}) collective-permute-start(bf16[16,16,128]{2,1,0:T(8,128)(2,1)S(1)} %all_to_all.5.mine_ref), channel_id=1, source_target_pairs={{0,4},{4,0},{8,12},{12,8},{16,20},{20,16},{24,28},{28,24},{1,5},{5... | collective-permute-start | bytes 196616 | tf_op jit(solution)/shard_map/ppermute | solution.py:251
where the time goes:
time: 17.9 us; the launch traced here: 17.7 us
  blocking collectives  12.2 us (68%)
  Pallas kernels  4.23 us (24%)
  waiting for transfers between devices  1.14 us (6%)
    all_to_all x1, blocking collectives, on_device(): lax.all_to_all(spectra, ('tile', 'chan'), split_axis=0, concat_axis=0, ax...  12.2 us
    pallas_call x1, Pallas kernels, on_device(): pl.pallas_call(functools.partial(front_kernel, own, chans, n_tile), out_s...  3.35 us
    ppermute x1, waiting for transfers between devices, on_device(): other = lax.ppermute(mine, 'chan', [(c, c ^ 1) for c in range(n_chan)])  1.14 us
    pallas_call x1, Pallas kernels, on_device(): pl.pallas_call(functools.partial(back_kernel, own, grid_side), out_shape=...  0.89 us
  transfers between devices with their start and end apart: 1, of which 1 were waited for; matrix products, arithmetic and copies ran while one was open for 0% of the time, Pallas kernels for 0%

commit v1 on v0

--- a/solution.py
+++ b/solution.py
@@ -140,7 +140,7 @@
                 turned[tap * kinds : (tap + 1) * kinds, :], turned.shape[1] - tap, axis=1
             )
             spectra = spectra + shifted[:, :SPECTRA_SUMMED]
-        spectra = spectra * mask_ref[0, i].astype(jnp.float32)
+        spectra = spectra * mask_ref[:, i : i + 1].astype(jnp.float32)
         for half in range(HALVES):
             for q in range(2):
                 block_ref[pl.ds((i * HALVES + half) * 2 + q, chans, stride=4 * own), :] = spectra[
@@ -230,7 +230,7 @@
         out_specs=vmem,
         scratch_shapes=[
             pltpu.VMEM((1, chans), jnp.int32),
-            pltpu.SMEM(input_good_mask.shape, jnp.int32),
+            pltpu.VMEM(input_good_mask.shape, jnp.int32),
             pltpu.VMEM(fir_taps.shape, jnp.float32),
             pltpu.VMEM((DIRECT, ROWS, own, LANES), jnp.bfloat16),
             pltpu.VMEM((ROWS, BLOCKS - DIRECT, own, LANES), jnp.bfloat16),

time: 17.9 us -> 17.9 us (level)
  no operation moved by 1% of the time
where the time goes in v1:
time: 17.9 us; the launch traced here: 17.7 us
  blocking collectives  12.2 us (68%)
  Pallas kernels  4.24 us (24%)
  waiting for transfers between devices  1.14 us (6%)
    all_to_all x1, blocking collectives, on_device(): lax.all_to_all(spectra, ('tile', 'chan'), split_axis=0, concat_axis=0, ax...  12.2 us
    pallas_call x1, Pallas kernels, on_device(): pl.pallas_call(functools.partial(front_kernel, own, chans, n_tile), out_s...  3.36 us
    ppermute x1, waiting for transfers between devices, on_device(): other = lax.ppermute(mine, 'chan', [(c, c ^ 1) for c in range(n_chan)])  1.14 us
    pallas_call x1, Pallas kernels, on_device(): pl.pallas_call(functools.partial(back_kernel, own, grid_side), out_shape=...  0.89 us
  transfers between devices with their start and end apart: 1, of which 1 were waited for; matrix products, arithmetic and copies ran while one was open for 0% of the time, Pallas kernels for 0%

profile of v1, /device:TPU:0, one launch (start us, length us, event | category | flops | bytes accessed | tf_op | source)
XLA Modules:
  0.0 17.7 jit_solution(13287091797892549684)
XLA Ops:
  0.0 0.0 copy-start
  0.0 3.4 %front.1 = bf16[4,64,128]{2,1,0:T(8,128)(2,1)S(1)} custom-call(s32[1,8]{1,0:T(1,128)} %bitcast.9, s32[1,2]{1,0:T(1,128)} %mask_hbm.1, f32[16,2048]{1,0:T(8,128)} %taps_hbm.1, bf16[271,16,2,128]{3,2,1,0:T(2,128)(2,1)} %bitcast.8), custom_call_target="tpu_custom_call" | custom-call | tf_op jit(solution)/shard_map/front/pallas_call | solution.py:226
  3.4 12.2 %all_to_all.5.mine_ref = bf16[16,16,128]{2,1,0:T(8,128)(2,1)S(1)} all-to-all(bf16[16,16,128]{2,1,0:T(8,128)(2,1)S(1)} %bitcast.6), channel_id=1, replica_groups={{31,0,12,20,24,5,9,17,29,2,14,22,26,7,11,19},{27,4,8,16,28,1,13,21,25,6..., dimensions={0} | all-to-all | bytes 131072 | tf_op jit(solution)/shard_map/all_to_all | solution.py:248
  15.6 0.1 collective-permute-start
  15.7 1.1 %collective-permute-done.other_ref = bf16[16,16,128]{2,1,0:T(8,128)(2,1)S(1)} collective-permute-done((bf16[16,16,128]{2,1,0:T(8,128)(2,1)S(1)}, bf16[16,16,128]{2,1,0:T(8,128)(2,1)S(1)}, u32[]{:S(2)}, u32[]{:S(2)}) %collective-permute-start) | collective-permute-done | bytes 65568 | tf_op jit(solution)/shard_map/ppermute | solution.py:251
  16.8 0.0 copy-done
  16.8 0.9 %back.1 = bf16[1,1,2,32,32]{4,3,2,1,0:T(8,128)(2,1)} custom-call(s32[4,8]{1,0:T(4,128)S(1)} %bitcast.7, bf16[16,16,128]{2,1,0:T(8,128)(2,1)S(1)} %all_to_all.5.mine_ref, bf16[16,16,128]{2,1,0:T(8,128)(2,1)S(1)} %collective-permute-done.other_ref), custom_call_target="tpu_custom_call" | custom-call | tf_op jit(solution)/shard_map/back/pallas_call | solution.py:255
Async XLA Ops:
  0.0 16.8 %copy-start = (s32[8,4]{0,1:T(4,128)S(1)}, s32[8,4]{0,1:T(4,128)}, u32[]{:S(2)}) copy-start(s32[8,4]{0,1:T(4,128)} %param.9) | copy-start | bytes 388
  15.6 1.3 %collective-permute-start = (bf16[16,16,128]{2,1,0:T(8,128)(2,1)S(1)}, bf16[16,16,128]{2,1,0:T(8,128)(2,1)S(1)}, u32[]{:S(2)}, u32[]{:S(2)}) collective-permute-start(bf16[16,16,128]{2,1,0:T(8,128)(2,1)S(1)} %all_to_all.5.mine_ref), channel_id=1, source_target_pairs={{0,4},{4,0},{8,12},{12,8},{16,20},{20,16},{24,28},{28,24},{1,5},{5... | collective-permute-start | bytes 196616 | tf_op jit(solution)/shard_map/ppermute | solution.py:251

commit v2 on v1

--- a/solution.py
+++ b/solution.py
@@ -61,13 +61,11 @@
     return [jnp.concatenate([cosine, -sine], axis=0) for cosine, sine in blocks]
 
 
-def build_table(chans, blocks, taps_ref, table_ref):
+def build_table(blocks, taps_ref, table_ref):
     for nb, dft in enumerate(blocks):
         columns = slice(nb * LANES, (nb + 1) * LANES)
-        for tap in range(FILTER_TAPS):
-            table_ref[tap * 2 * chans : (tap + 1) * 2 * chans, columns] = (
-                dft * taps_ref[tap : tap + 1, columns]
-            ).astype(jnp.bfloat16)
+        scaled = [dft * taps_ref[tap : tap + 1, columns] for tap in range(FILTER_TAPS)]
+        table_ref[columns, :] = jnp.concatenate(scaled, axis=0).astype(jnp.bfloat16).T
 
 
 def front_kernel(
@@ -102,7 +100,7 @@
     blocks = dft_blocks(chans, channels_ref)
     small[0].wait()
     small[2].wait()
-    build_table(chans, blocks, taps_ref, table_ref)
+    build_table(blocks, taps_ref, table_ref)
     for part, transfer in enumerate(rest):
         transfer.wait()
         frames = pl.ds(part * (ROWS // 2), ROWS // 2)
@@ -119,7 +117,7 @@
             axis=1,
         ),
         table_ref[...],
-        (((1,), (1,)), ((), ())),
+        (((1,), (0,)), ((), ())),
         preferred_element_type=jnp.float32,
     )
     kinds = 2 * chans
@@ -235,7 +233,7 @@
             pltpu.VMEM((DIRECT, ROWS, own, LANES), jnp.bfloat16),
             pltpu.VMEM((ROWS, BLOCKS - DIRECT, own, LANES), jnp.bfloat16),
             pltpu.VMEM((BLOCKS - DIRECT, ROWS * own, LANES), jnp.bfloat16),
-            pltpu.VMEM((FILTER_TAPS * kinds, TRANSFORM_LENGTH), jnp.bfloat16),
+            pltpu.VMEM((TRANSFORM_LENGTH, FILTER_TAPS * kinds), jnp.bfloat16),
             pltpu.VMEM((own * folded_rows, LANES), jnp.float32),
             pltpu.VMEM((chans * per_block, LANES), jnp.float32),
             pltpu.SemaphoreType.DMA((DIRECT + 2,)),

time: 17.9 us -> 17.9 us (level)
  no operation moved by 1% of the time
where the time goes in v2:
time: 17.9 us; the launch traced here: 17.8 us
  blocking collectives  12.2 us (68%)
  Pallas kernels  4.27 us (24%)
  waiting for transfers between devices  1.14 us (6%)
    all_to_all x1, blocking collectives, on_device(): lax.all_to_all(spectra, ('tile', 'chan'), split_axis=0, concat_axis=0, ax...  12.2 us
    pallas_call x1, Pallas kernels, on_device(): pl.pallas_call(functools.partial(front_kernel, own, chans, n_tile), out_s...  3.39 us
    ppermute x1, waiting for transfers between devices, on_device(): other = lax.ppermute(mine, 'chan', [(c, c ^ 1) for c in range(n_chan)])  1.14 us
    pallas_call x1, Pallas kernels, on_device(): pl.pallas_call(functools.partial(back_kernel, own, grid_side), out_shape=...  0.88 us
  transfers between devices with their start and end apart: 1, of which 1 were waited for; matrix products, arithmetic and copies ran while one was open for 0% of the time, Pallas kernels for 0%

profile of v2, /device:TPU:0, one launch (start us, length us, event | category | flops | bytes accessed | tf_op | source)
XLA Modules:
  0.0 17.8 jit_solution(8197757890533804792)
XLA Ops:
  0.0 0.0 copy-start
  0.0 3.4 %front.1 = bf16[4,64,128]{2,1,0:T(8,128)(2,1)S(1)} custom-call(s32[1,8]{1,0:T(1,128)} %bitcast.9, s32[1,2]{1,0:T(1,128)} %mask_hbm.1, f32[16,2048]{1,0:T(8,128)} %taps_hbm.1, bf16[271,16,2,128]{3,2,1,0:T(2,128)(2,1)} %bitcast.8), custom_call_target="tpu_custom_call" | custom-call | tf_op jit(solution)/shard_map/front/pallas_call | solution.py:224
  3.4 12.2 %all_to_all.5.mine_ref = bf16[16,16,128]{2,1,0:T(8,128)(2,1)S(1)} all-to-all(bf16[16,16,128]{2,1,0:T(8,128)(2,1)S(1)} %bitcast.6), channel_id=1, replica_groups={{31,0,12,20,24,5,9,17,29,2,14,22,26,7,11,19},{27,4,8,16,28,1,13,21,25,6..., dimensions={0} | all-to-all | bytes 131072 | tf_op jit(solution)/shard_map/all_to_all | solution.py:246
  15.6 0.1 collective-permute-start
  15.7 1.1 %collective-permute-done.other_ref = bf16[16,16,128]{2,1,0:T(8,128)(2,1)S(1)} collective-permute-done((bf16[16,16,128]{2,1,0:T(8,128)(2,1)S(1)}, bf16[16,16,128]{2,1,0:T(8,128)(2,1)S(1)}, u32[]{:S(2)}, u32[]{:S(2)}) %collective-permute-start) | collective-permute-done | bytes 65568 | tf_op jit(solution)/shard_map/ppermute | solution.py:249
  16.9 0.0 copy-done
  16.9 0.9 %back.1 = bf16[1,1,2,32,32]{4,3,2,1,0:T(8,128)(2,1)} custom-call(s32[4,8]{1,0:T(4,128)S(1)} %bitcast.7, bf16[16,16,128]{2,1,0:T(8,128)(2,1)S(1)} %all_to_all.5.mine_ref, bf16[16,16,128]{2,1,0:T(8,128)(2,1)S(1)} %collective-permute-done.other_ref), custom_call_target="tpu_custom_call" | custom-call | tf_op jit(solution)/shard_map/back/pallas_call | solution.py:253
Async XLA Ops:
  0.0 16.9 %copy-start = (s32[8,4]{0,1:T(4,128)S(1)}, s32[8,4]{0,1:T(4,128)}, u32[]{:S(2)}) copy-start(s32[8,4]{0,1:T(4,128)} %param.9) | copy-start | bytes 388
  15.6 1.3 %collective-permute-start = (bf16[16,16,128]{2,1,0:T(8,128)(2,1)S(1)}, bf16[16,16,128]{2,1,0:T(8,128)(2,1)S(1)}, u32[]{:S(2)}, u32[]{:S(2)}) collective-permute-start(bf16[16,16,128]{2,1,0:T(8,128)(2,1)S(1)} %all_to_all.5.mine_ref), channel_id=1, source_target_pairs={{0,4},{4,0},{8,12},{12,8},{16,20},{20,16},{24,28},{28,24},{1,5},{5... | collective-permute-start | bytes 196616 | tf_op jit(solution)/shard_map/ppermute | solution.py:249

commit v3 on v1

--- a/solution.py
+++ b/solution.py
@@ -131,15 +131,14 @@
         folded = folded + product[
             start : start + kept * own, group * LANES : (group + 1) * LANES
         ]
-    fold_ref[: kept * own, :] = folded
+    fold_ref[...] = folded
     for i in range(own):
-        turned = fold_ref[pl.ds(i, fold_ref.shape[0] // own, stride=own), :].T
+        turned = fold_ref[pl.ds(i, kept, stride=own), :].T
         spectra = turned[:kinds, :SPECTRA_SUMMED]
         for tap in range(1, together):
-            shifted = pltpu.roll(
-                turned[tap * kinds : (tap + 1) * kinds, :], turned.shape[1] - tap, axis=1
-            )
-            spectra = spectra + shifted[:, :SPECTRA_SUMMED]
+            spectra = spectra + turned[
+                tap * kinds : (tap + 1) * kinds, tap : tap + SPECTRA_SUMMED
+            ]
         spectra = spectra * mask_ref[:, i : i + 1].astype(jnp.float32)
         for half in range(HALVES):
             for q in range(2):
@@ -222,7 +221,7 @@
     vmem = pl.BlockSpec(memory_space=pltpu.VMEM)
     per_block = 2 * HALVES * own
     kinds = 2 * chans
-    folded_rows = SPECTRA_SUMMED + (LANES if kinds < LANES else 0)
+    folded_rows = -(-(SPECTRA_SUMMED + LANES // kinds - 1) // 8) * 8
     spectra = pl.pallas_call(
         functools.partial(front_kernel, own, chans, n_tile),
         out_shape=pltpu.VMEM((n_tile, chans * per_block, LANES), jnp.bfloat16),

time: 17.9 us -> 17.9 us (level)
  no operation moved by 1% of the time
where the time goes in v3:
time: 17.9 us; the launch traced here: 17.7 us
  blocking collectives  12.2 us (68%)
  Pallas kernels  4.27 us (24%)
  waiting for transfers between devices  1.14 us (6%)
    all_to_all x1, blocking collectives, on_device(): lax.all_to_all(spectra, ('tile', 'chan'), split_axis=0, concat_axis=0, ax...  12.2 us
    pallas_call x1, Pallas kernels, on_device(): pl.pallas_call(functools.partial(front_kernel, own, chans, n_tile), out_s...  3.38 us
    ppermute x1, waiting for transfers between devices, on_device(): other = lax.ppermute(mine, 'chan', [(c, c ^ 1) for c in range(n_chan)])  1.14 us
    pallas_call x1, Pallas kernels, on_device(): pl.pallas_call(functools.partial(back_kernel, own, grid_side), out_shape=...  0.89 us
  transfers between devices with their start and end apart: 1, of which 1 were waited for; matrix products, arithmetic and copies ran while one was open for 0% of the time, Pallas kernels for 0%

profile of v3, /device:TPU:0, one launch (start us, length us, event | category | flops | bytes accessed | tf_op | source)
XLA Modules:
  0.0 17.7 jit_solution(8888022498812749378)
XLA Ops:
  0.0 0.0 copy-start
  0.0 3.4 %front.1 = bf16[4,64,128]{2,1,0:T(8,128)(2,1)S(1)} custom-call(s32[1,8]{1,0:T(1,128)} %bitcast.9, s32[1,2]{1,0:T(1,128)} %mask_hbm.1, f32[16,2048]{1,0:T(8,128)} %taps_hbm.1, bf16[271,16,2,128]{3,2,1,0:T(2,128)(2,1)} %bitcast.8), custom_call_target="tpu_custom_call" | custom-call | tf_op jit(solution)/shard_map/front/pallas_call | solution.py:225
  3.4 12.2 %all_to_all.5.mine_ref = bf16[16,16,128]{2,1,0:T(8,128)(2,1)S(1)} all-to-all(bf16[16,16,128]{2,1,0:T(8,128)(2,1)S(1)} %bitcast.6), channel_id=1, replica_groups={{31,0,12,20,24,5,9,17,29,2,14,22,26,7,11,19},{27,4,8,16,28,1,13,21,25,6..., dimensions={0} | all-to-all | bytes 131072 | tf_op jit(solution)/shard_map/all_to_all | solution.py:247
  15.6 0.1 collective-permute-start
  15.7 1.1 %collective-permute-done.other_ref = bf16[16,16,128]{2,1,0:T(8,128)(2,1)S(1)} collective-permute-done((bf16[16,16,128]{2,1,0:T(8,128)(2,1)S(1)}, bf16[16,16,128]{2,1,0:T(8,128)(2,1)S(1)}, u32[]{:S(2)}, u32[]{:S(2)}) %collective-permute-start) | collective-permute-done | bytes 65568 | tf_op jit(solution)/shard_map/ppermute | solution.py:250
  16.9 0.0 copy-done
  16.9 0.9 %back.1 = bf16[1,1,2,32,32]{4,3,2,1,0:T(8,128)(2,1)} custom-call(s32[4,8]{1,0:T(4,128)S(1)} %bitcast.7, bf16[16,16,128]{2,1,0:T(8,128)(2,1)S(1)} %all_to_all.5.mine_ref, bf16[16,16,128]{2,1,0:T(8,128)(2,1)S(1)} %collective-permute-done.other_ref), custom_call_target="tpu_custom_call" | custom-call | tf_op jit(solution)/shard_map/back/pallas_call | solution.py:254
Async XLA Ops:
  0.0 16.9 %copy-start = (s32[8,4]{0,1:T(4,128)S(1)}, s32[8,4]{0,1:T(4,128)}, u32[]{:S(2)}) copy-start(s32[8,4]{0,1:T(4,128)} %param.9) | copy-start | bytes 388
  15.6 1.3 %collective-permute-start = (bf16[16,16,128]{2,1,0:T(8,128)(2,1)S(1)}, bf16[16,16,128]{2,1,0:T(8,128)(2,1)S(1)}, u32[]{:S(2)}, u32[]{:S(2)}) collective-permute-start(bf16[16,16,128]{2,1,0:T(8,128)(2,1)S(1)} %all_to_all.5.mine_ref), channel_id=1, source_target_pairs={{0,4},{4,0},{8,12},{12,8},{16,20},{20,16},{24,28},{28,24},{1,5},{5... | collective-permute-start | bytes 196616 | tf_op jit(solution)/shard_map/ppermute | solution.py:250

commit v4 on v1

--- a/solution.py
+++ b/solution.py
@@ -16,6 +16,7 @@
 LANES = 128
 BLOCKS = TRANSFORM_LENGTH // LANES
 DIRECT = 10
+EARLY = 5
 HALVES = SPECTRA_SUMMED // LANES
 OCTANT = TRANSFORM_LENGTH // 8
 
@@ -96,12 +97,14 @@
     ]
     for transfer in small:
         transfer.start()
-    for place, transfer in enumerate(rest + transfers):
+    for place, transfer in enumerate(rest + transfers[:EARLY]):
         transfer.start(priority=place % 2)
     small[1].wait()
     blocks = dft_blocks(chans, channels_ref)
     small[0].wait()
     small[2].wait()
+    for place, transfer in enumerate(transfers[EARLY:]):
+        transfer.start(priority=place % 2)
     build_table(chans, blocks, taps_ref, table_ref)
     for part, transfer in enumerate(rest):
         transfer.wait()
@@ -110,17 +113,26 @@
         for place in range(BLOCKS - DIRECT):
             sorted_ref[place, lines, :] = rest_ref[frames, place].reshape(ROWS // 2 * own, LANES)
     rows_ref = x_ref.reshape(DIRECT, ROWS * own, LANES)
-    for transfer in transfers:
+
+    def product_of(parts, *columns):
+        table = jnp.concatenate([table_ref[:, part] for part in columns], axis=1)
+        return lax.dot_general(
+            jnp.concatenate(parts, axis=1), table, (((1,), (1,)), ((), ())),
+            preferred_element_type=jnp.float32,
+        )
+
+    for transfer in transfers[:EARLY]:
         transfer.wait()
-    product = lax.dot_general(
-        jnp.concatenate(
-            [rows_ref[nb] for nb in range(DIRECT)]
-            + [sorted_ref[place] for place in range(BLOCKS - DIRECT)],
-            axis=1,
-        ),
-        table_ref[...],
-        (((1,), (1,)), ((), ())),
-        preferred_element_type=jnp.float32,
+    product = product_of(
+        [rows_ref[nb] for nb in range(EARLY)]
+        + [sorted_ref[place] for place in range(BLOCKS - DIRECT)],
+        slice(0, EARLY * LANES),
+        slice(DIRECT * LANES, BLOCKS * LANES),
+    )
+    for transfer in transfers[EARLY:]:
+        transfer.wait()
+    product = product + product_of(
+        [rows_ref[nb] for nb in range(EARLY, DIRECT)], slice(EARLY * LANES, DIRECT * LANES)
     )
     kinds = 2 * chans
     together = LANES // kinds

time: 17.9 us -> 18.3 us (1.022)
  Pallas kernels: 4.24 us -> 4.59 us
    pallas_call x1, Pallas kernels: 3.36 us -> 3.71 us  [on_device(): pl.pallas_call(functools.partial(front_kernel, own, chans, n_tile), out_s...]
where the time goes in v4:
time: 18.3 us; the launch traced here: 18.1 us
  blocking collectives  12.2 us (67%)
  Pallas kernels  4.59 us (25%)
  waiting for transfers between devices  1.14 us (6%)
    all_to_all x1, blocking collectives, on_device(): lax.all_to_all(spectra, ('tile', 'chan'), split_axis=0, concat_axis=0, ax...  12.2 us
    pallas_call x1, Pallas kernels, on_device(): pl.pallas_call(functools.partial(front_kernel, own, chans, n_tile), out_s...  3.71 us
    ppermute x1, waiting for transfers between devices, on_device(): other = lax.ppermute(mine, 'chan', [(c, c ^ 1) for c in range(n_chan)])  1.14 us
    pallas_call x1, Pallas kernels, on_device(): pl.pallas_call(functools.partial(back_kernel, own, grid_side), out_shape=...  0.88 us
  transfers between devices with their start and end apart: 1, of which 1 were waited for; matrix products, arithmetic and copies ran while one was open for 0% of the time, Pallas kernels for 0%

profile of v4, /device:TPU:0, one launch (start us, length us, event | category | flops | bytes accessed | tf_op | source)
XLA Modules:
  0.0 18.1 jit_solution(10502050966062183234)
XLA Ops:
  0.0 0.0 copy-start
  0.0 3.7 %front.1 = bf16[4,64,128]{2,1,0:T(8,128)(2,1)S(1)} custom-call(s32[1,8]{1,0:T(1,128)} %bitcast.9, s32[1,2]{1,0:T(1,128)} %mask_hbm.1, f32[16,2048]{1,0:T(8,128)} %taps_hbm.1, bf16[271,16,2,128]{3,2,1,0:T(2,128)(2,1)} %bitcast.8), custom_call_target="tpu_custom_call" | custom-call | tf_op jit(solution)/shard_map/front/pallas_call | solution.py:238
  3.7 12.2 %all_to_all.5.mine_ref = bf16[16,16,128]{2,1,0:T(8,128)(2,1)S(1)} all-to-all(bf16[16,16,128]{2,1,0:T(8,128)(2,1)S(1)} %bitcast.6), channel_id=1, replica_groups={{31,0,12,20,24,5,9,17,29,2,14,22,26,7,11,19},{27,4,8,16,28,1,13,21,25,6..., dimensions={0} | all-to-all | bytes 131072 | tf_op jit(solution)/shard_map/all_to_all | solution.py:260
  15.9 0.1 collective-permute-start
  16.0 1.1 %collective-permute-done.other_ref = bf16[16,16,128]{2,1,0:T(8,128)(2,1)S(1)} collective-permute-done((bf16[16,16,128]{2,1,0:T(8,128)(2,1)S(1)}, bf16[16,16,128]{2,1,0:T(8,128)(2,1)S(1)}, u32[]{:S(2)}, u32[]{:S(2)}) %collective-permute-start) | collective-permute-done | bytes 65568 | tf_op jit(solution)/shard_map/ppermute | solution.py:263
  17.2 0.0 copy-done
  17.2 0.9 %back.1 = bf16[1,1,2,32,32]{4,3,2,1,0:T(8,128)(2,1)} custom-call(s32[4,8]{1,0:T(4,128)S(1)} %bitcast.7, bf16[16,16,128]{2,1,0:T(8,128)(2,1)S(1)} %all_to_all.5.mine_ref, bf16[16,16,128]{2,1,0:T(8,128)(2,1)S(1)} %collective-permute-done.other_ref), custom_call_target="tpu_custom_call" | custom-call | tf_op jit(solution)/shard_map/back/pallas_call | solution.py:267
Async XLA Ops:
  0.0 17.2 %copy-start = (s32[8,4]{0,1:T(4,128)S(1)}, s32[8,4]{0,1:T(4,128)}, u32[]{:S(2)}) copy-start(s32[8,4]{0,1:T(4,128)} %param.9) | copy-start | bytes 388
  15.9 1.3 %collective-permute-start = (bf16[16,16,128]{2,1,0:T(8,128)(2,1)S(1)}, bf16[16,16,128]{2,1,0:T(8,128)(2,1)S(1)}, u32[]{:S(2)}, u32[]{:S(2)}) collective-permute-start(bf16[16,16,128]{2,1,0:T(8,128)(2,1)S(1)} %all_to_all.5.mine_ref), channel_id=1, source_target_pairs={{0,4},{4,0},{8,12},{12,8},{16,20},{20,16},{24,28},{28,24},{1,5},{5... | collective-permute-start | bytes 196616 | tf_op jit(solution)/shard_map/ppermute | solution.py:263

commit v5 on v1

--- a/solution.py
+++ b/solution.py
@@ -94,10 +94,10 @@
         )
         for part, (start, stop) in enumerate(halves)
     ]
+    for place, transfer in enumerate(rest + transfers):
+        transfer.start(priority=place % 2)
     for transfer in small:
         transfer.start()
-    for place, transfer in enumerate(rest + transfers):
-        transfer.start(priority=place % 2)
     small[1].wait()
     blocks = dft_blocks(chans, channels_ref)
     small[0].wait()

time: 17.9 us -> 17.9 us (level)
  no operation moved by 1% of the time
where the time goes in v5:
time: 17.9 us; the launch traced here: 17.7 us
  blocking collectives  12.2 us (68%)
  Pallas kernels  4.24 us (24%)
  waiting for transfers between devices  1.14 us (6%)
    all_to_all x1, blocking collectives, on_device(): lax.all_to_all(spectra, ('tile', 'chan'), split_axis=0, concat_axis=0, ax...  12.2 us
    pallas_call x1, Pallas kernels, on_device(): pl.pallas_call(functools.partial(front_kernel, own, chans, n_tile), out_s...  3.36 us
    ppermute x1, waiting for transfers between devices, on_device(): other = lax.ppermute(mine, 'chan', [(c, c ^ 1) for c in range(n_chan)])  1.14 us
    pallas_call x1, Pallas kernels, on_device(): pl.pallas_call(functools.partial(back_kernel, own, grid_side), out_shape=...  0.89 us
  transfers between devices with their start and end apart: 1, of which 1 were waited for; matrix products, arithmetic and copies ran while one was open for 0% of the time, Pallas kernels for 0%

profile of v5, /device:TPU:0, one launch (start us, length us, event | category | flops | bytes accessed | tf_op | source)
XLA Modules:
  0.0 17.7 jit_solution(10058918829401403677)
XLA Ops:
  0.0 0.0 copy-start
  0.0 3.4 %front.1 = bf16[4,64,128]{2,1,0:T(8,128)(2,1)S(1)} custom-call(s32[1,8]{1,0:T(1,128)} %bitcast.9, s32[1,2]{1,0:T(1,128)} %mask_hbm.1, f32[16,2048]{1,0:T(8,128)} %taps_hbm.1, bf16[271,16,2,128]{3,2,1,0:T(2,128)(2,1)} %bitcast.8), custom_call_target="tpu_custom_call" | custom-call | tf_op jit(solution)/shard_map/front/pallas_call | solution.py:226
  3.4 12.2 %all_to_all.5.mine_ref = bf16[16,16,128]{2,1,0:T(8,128)(2,1)S(1)} all-to-all(bf16[16,16,128]{2,1,0:T(8,128)(2,1)S(1)} %bitcast.6), channel_id=1, replica_groups={{31,0,12,20,24,5,9,17,29,2,14,22,26,7,11,19},{27,4,8,16,28,1,13,21,25,6..., dimensions={0} | all-to-all | bytes 131072 | tf_op jit(solution)/shard_map/all_to_all | solution.py:248
  15.6 0.1 collective-permute-start
  15.7 1.1 %collective-permute-done.other_ref = bf16[16,16,128]{2,1,0:T(8,128)(2,1)S(1)} collective-permute-done((bf16[16,16,128]{2,1,0:T(8,128)(2,1)S(1)}, bf16[16,16,128]{2,1,0:T(8,128)(2,1)S(1)}, u32[]{:S(2)}, u32[]{:S(2)}) %collective-permute-start) | collective-permute-done | bytes 65568 | tf_op jit(solution)/shard_map/ppermute | solution.py:251
  16.8 0.0 copy-done
  16.8 0.9 %back.1 = bf16[1,1,2,32,32]{4,3,2,1,0:T(8,128)(2,1)} custom-call(s32[4,8]{1,0:T(4,128)S(1)} %bitcast.7, bf16[16,16,128]{2,1,0:T(8,128)(2,1)S(1)} %all_to_all.5.mine_ref, bf16[16,16,128]{2,1,0:T(8,128)(2,1)S(1)} %collective-permute-done.other_ref), custom_call_target="tpu_custom_call" | custom-call | tf_op jit(solution)/shard_map/back/pallas_call | solution.py:255
Async XLA Ops:
  0.0 16.8 %copy-start = (s32[8,4]{0,1:T(4,128)S(1)}, s32[8,4]{0,1:T(4,128)}, u32[]{:S(2)}) copy-start(s32[8,4]{0,1:T(4,128)} %param.9) | copy-start | bytes 388
  15.6 1.3 %collective-permute-start = (bf16[16,16,128]{2,1,0:T(8,128)(2,1)S(1)}, bf16[16,16,128]{2,1,0:T(8,128)(2,1)S(1)}, u32[]{:S(2)}, u32[]{:S(2)}) collective-permute-start(bf16[16,16,128]{2,1,0:T(8,128)(2,1)S(1)} %all_to_all.5.mine_ref), channel_id=1, source_target_pairs={{0,4},{4,0},{8,12},{12,8},{16,20},{20,16},{24,28},{28,24},{1,5},{5... | collective-permute-start | bytes 196616 | tf_op jit(solution)/shard_map/ppermute | solution.py:251

commit v6 on v5

--- a/solution.py
+++ b/solution.py
@@ -15,7 +15,7 @@
 ROWS = 272
 LANES = 128
 BLOCKS = TRANSFORM_LENGTH // LANES
-DIRECT = 10
+DIRECT = 8
 HALVES = SPECTRA_SUMMED // LANES
 OCTANT = TRANSFORM_LENGTH // 8
 

time: 17.9 us -> 17.9 us (level)
  no operation moved by 1% of the time
where the time goes in v6:
time: 17.9 us; the launch traced here: 17.7 us
  blocking collectives  12.2 us (68%)
  Pallas kernels  4.25 us (24%)
  waiting for transfers between devices  1.14 us (6%)
    all_to_all x1, blocking collectives, on_device(): lax.all_to_all(spectra, ('tile', 'chan'), split_axis=0, concat_axis=0, ax...  12.2 us
    pallas_call x1, Pallas kernels, on_device(): pl.pallas_call(functools.partial(front_kernel, own, chans, n_tile), out_s...  3.36 us
    ppermute x1, waiting for transfers between devices, on_device(): other = lax.ppermute(mine, 'chan', [(c, c ^ 1) for c in range(n_chan)])  1.14 us
    pallas_call x1, Pallas kernels, on_device(): pl.pallas_call(functools.partial(back_kernel, own, grid_side), out_shape=...  0.89 us
  transfers between devices with their start and end apart: 1, of which 1 were waited for; matrix products, arithmetic and copies ran while one was open for 0% of the time, Pallas kernels for 0%

profile of v6, /device:TPU:0, one launch (start us, length us, event | category | flops | bytes accessed | tf_op | source)
XLA Modules:
  0.0 17.7 jit_solution(1338182217098593486)
XLA Ops:
  0.0 0.0 copy-start
  0.0 3.4 %front.1 = bf16[4,64,128]{2,1,0:T(8,128)(2,1)S(1)} custom-call(s32[1,8]{1,0:T(1,128)} %bitcast.9, s32[1,2]{1,0:T(1,128)} %mask_hbm.1, f32[16,2048]{1,0:T(8,128)} %taps_hbm.1, bf16[271,16,2,128]{3,2,1,0:T(2,128)(2,1)} %bitcast.8), custom_call_target="tpu_custom_call" | custom-call | tf_op jit(solution)/shard_map/front/pallas_call | solution.py:226
  3.4 12.2 %all_to_all.5.mine_ref = bf16[16,16,128]{2,1,0:T(8,128)(2,1)S(1)} all-to-all(bf16[16,16,128]{2,1,0:T(8,128)(2,1)S(1)} %bitcast.6), channel_id=1, replica_groups={{31,0,12,20,24,5,9,17,29,2,14,22,26,7,11,19},{27,4,8,16,28,1,13,21,25,6..., dimensions={0} | all-to-all | bytes 131072 | tf_op jit(solution)/shard_map/all_to_all | solution.py:248
  15.6 0.1 collective-permute-start
  15.7 1.1 %collective-permute-done.other_ref = bf16[16,16,128]{2,1,0:T(8,128)(2,1)S(1)} collective-permute-done((bf16[16,16,128]{2,1,0:T(8,128)(2,1)S(1)}, bf16[16,16,128]{2,1,0:T(8,128)(2,1)S(1)}, u32[]{:S(2)}, u32[]{:S(2)}) %collective-permute-start) | collective-permute-done | bytes 65568 | tf_op jit(solution)/shard_map/ppermute | solution.py:251
  16.8 0.0 copy-done
  16.8 0.9 %back.1 = bf16[1,1,2,32,32]{4,3,2,1,0:T(8,128)(2,1)} custom-call(s32[4,8]{1,0:T(4,128)S(1)} %bitcast.7, bf16[16,16,128]{2,1,0:T(8,128)(2,1)S(1)} %all_to_all.5.mine_ref, bf16[16,16,128]{2,1,0:T(8,128)(2,1)S(1)} %collective-permute-done.other_ref), custom_call_target="tpu_custom_call" | custom-call | tf_op jit(solution)/shard_map/back/pallas_call | solution.py:255
Async XLA Ops:
  0.0 16.8 %copy-start = (s32[8,4]{0,1:T(4,128)S(1)}, s32[8,4]{0,1:T(4,128)}, u32[]{:S(2)}) copy-start(s32[8,4]{0,1:T(4,128)} %param.9) | copy-start | bytes 388
  15.6 1.3 %collective-permute-start = (bf16[16,16,128]{2,1,0:T(8,128)(2,1)S(1)}, bf16[16,16,128]{2,1,0:T(8,128)(2,1)S(1)}, u32[]{:S(2)}, u32[]{:S(2)}) collective-permute-start(bf16[16,16,128]{2,1,0:T(8,128)(2,1)S(1)} %all_to_all.5.mine_ref), channel_id=1, source_target_pairs={{0,4},{4,0},{8,12},{12,8},{16,20},{20,16},{24,28},{28,24},{1,5},{5... | collective-permute-start | bytes 196616 | tf_op jit(solution)/shard_map/ppermute | solution.py:251
